TPU v7x, 256 devices: a whole 4x4x8 slice. The times are simulated.
256 devices in a mesh: dp: 128 (over z, x, y), pair: 2 (over core).
Axes of the slice: x: 4, y: 4, z: 8, core: 2. Of those that a mesh axis runs over, the one named last changes fastest.
Arguments:
- hidden_in: bfloat16 [32768, 1536], P(('dp', 'pair')), may hold values from -24 to 24
- segment_ids: int32 [32768], replicated, may hold values from 0 to 511, as said below
- frame_mask: int32 [32768], P(('dp', 'pair')), may hold values from 0 to 1, as said below
- dw_kernel: float32 [31, 1536], P(None, ('dp', 'pair')), may hold values from -1 to 1
- norm_scale: float32 [1536], P(('dp', 'pair')), may hold values from 0.1 to 1.9
- norm_shift: float32 [1536], P(('dp', 'pair')), may hold values from -3 to 3
- out_weight: bfloat16 [1536, 1536], P(('dp', 'pair')), may hold values from -0.15625 to 0.15625
- cotangent: bfloat16 [32768, 1536], P(('dp', 'pair')), may hold values from -6 to 6
Outputs:
- module_out: bfloat16 [32768, 1536], P(('dp', 'pair'))
- grad_hidden: bfloat16 [32768, 1536], P(('dp', 'pair'))
- grad_kernel: float32 [31, 1536], P(None, ('dp', 'pair'))
- grad_scale: float32 [1536], P(('dp', 'pair'))
- grad_shift: float32 [1536], P(('dp', 'pair'))
- grad_weight: float32 [1536, 1536], P(('dp', 'pair'))
Inputs may be any that keep to these rules, and one draw needn't show every extreme that they name: `segment_ids`: non-falling along the stream, starting at 0; each utterance has 1 to 192 frames; no utterance begins at a frame whose index is a positive multiple of 128. `frame_mask`: 1 on every frame whose index modulo 16 is 0 or 15.
All inputs are finite; a program needn't handle non-finite values.
Results may differ from a plain program's by a relative error of at most 0.0049.
Values may be sent and summed in bfloat16 or wider, within the bound.
No kernel may reach another device: no remote copies, remote signals or barrier semaphores. Data moves between devices by JAX's collectives and lax.ppermute only.
A program may use at most 128 MiB of HBM per device.

v0:
```python
import jax
import jax.numpy as jnp
from jax import lax
from jax.sharding import PartitionSpec as P

KERNEL = 31


def padded(cells, sides, width):
    for axis, dim in sides:
        count = lax.axis_size(axis)
        ends = count - 1
        head = lax.slice_in_dim(cells, 0, width, axis=dim)
        tail = lax.slice_in_dim(cells, cells.shape[dim] - width, cells.shape[dim], axis=dim)
        cells = jnp.concatenate(
            [
                lax.ppermute(tail, axis, [(i, (i + 1) % count) for i in range(ends)]),
                cells,
                lax.ppermute(head, axis, [((i + 1) % count, i) for i in range(ends)]),
            ],
            axis=dim,
        )
    return cells


def local(
    hidden_in, segment_ids, frame_mask, dw_kernel, norm_scale, norm_shift, out_weight, cotangent
):
    local_rows = hidden_in.shape[0]
    shard_cols = norm_scale.shape[0]
    half = KERNEL // 2
    device_pos = lax.axis_index(("dp", "pair"))
    weight_col = frame_mask.astype(jnp.float32)[:, None]
    stacked = jnp.concatenate([dw_kernel, norm_scale[None, :], norm_shift[None, :]], axis=0)
    params_full = lax.all_gather(stacked, ("dp", "pair"), axis=1, tiled=True)
    kernel_full = params_full[:KERNEL]
    scale_full = params_full[KERNEL]
    shift_full = params_full[KERNEL + 1]
    seg_pad = jnp.pad(segment_ids, (half, half), constant_values=-1)
    seg_local = lax.dynamic_slice_in_dim(seg_pad, device_pos * local_rows, local_rows + 2 * half)
    own_seg = seg_local[half : half + local_rows]
    masked = jnp.where(frame_mask[:, None] == 1, hidden_in, jnp.zeros_like(hidden_in))
    padded_in = padded(masked, ((("dp", "pair"), 0),), half).astype(jnp.float32)
    conv = jnp.zeros((local_rows, params_full.shape[1]), jnp.float32)
    for offset in range(KERNEL):
        same_seg = (seg_local[offset : offset + local_rows] == own_seg)[:, None]
        conv = conv + jnp.where(
            same_seg, kernel_full[offset] * padded_in[offset : offset + local_rows], 0.0
        )
    total, count = lax.psum(
        (jnp.sum(weight_col * conv, axis=0), jnp.sum(weight_col)), ("dp", "pair")
    )
    mean = total / count
    centred = conv - mean
    spread = lax.psum(jnp.sum(weight_col * centred * centred, axis=0), ("dp", "pair"))
    variance = spread / count
    inv_std = lax.rsqrt(variance + 1e-05)
    normed = centred * inv_std
    pre = scale_full * normed + shift_full
    sig = jax.nn.sigmoid(pre)
    act = (weight_col * pre * sig).astype(jnp.bfloat16)
    weight_full = lax.all_gather(out_weight, ("dp", "pair"), axis=0, tiled=True)
    module_out = jnp.dot(act, weight_full, preferred_element_type=jnp.float32).astype(jnp.bfloat16)
    grad_act = lax.dot_general(
        cotangent, weight_full, (((1,), (1,)), ((), ())), preferred_element_type=jnp.float32
    )
    grad_pre = weight_col * grad_act * sig * (1.0 + pre * (1.0 - sig))
    scale_sum, shift_sum = lax.psum(
        (jnp.sum(grad_pre * normed, axis=0), jnp.sum(grad_pre, axis=0)), ("dp", "pair")
    )
    col_start = device_pos * shard_cols
    grad_scale = lax.dynamic_slice_in_dim(scale_sum, col_start, shard_cols)
    grad_shift = lax.dynamic_slice_in_dim(shift_sum, col_start, shard_cols)
    grad_conv = (
        weight_col
        * scale_full
        * inv_std
        * (grad_pre - shift_sum / count - normed * scale_sum / count)
    )
    grad_pad = padded(grad_conv, ((("dp", "pair"), 0),), half)
    grad_local = jnp.zeros_like(grad_conv)
    tap_rows = []
    for offset in range(KERNEL):
        same_fwd = (seg_local[offset : offset + local_rows] == own_seg)[:, None]
        tap_rows.append(
            jnp.sum(
                jnp.where(same_fwd, grad_conv * padded_in[offset : offset + local_rows], 0.0),
                axis=0,
            )
        )
        back = 2 * half - offset
        same_back = (seg_local[back : back + local_rows] == own_seg)[:, None]
        grad_local = grad_local + jnp.where(
            same_back, kernel_full[offset] * grad_pad[back : back + local_rows], 0.0
        )
    grad_kernel = lax.psum_scatter(
        jnp.stack(tap_rows, axis=0), ("dp", "pair"), scatter_dimension=1, tiled=True
    )
    grad_hidden = (weight_col * grad_local).astype(jnp.bfloat16)
    grad_weight = lax.psum_scatter(
        lax.dot_general(
            act, cotangent, (((0,), (0,)), ((), ())), preferred_element_type=jnp.float32
        ),
        ("dp", "pair"),
        scatter_dimension=0,
        tiled=True,
    )
    return (module_out, grad_hidden, grad_kernel, grad_scale, grad_shift, grad_weight)


def solution(mesh):
    return jax.shard_map(
        local,
        mesh=mesh,
        in_specs=(
            P(("dp", "pair"), None),
            P(),
            P(("dp", "pair")),
            P(None, ("dp", "pair")),
            P(("dp", "pair")),
            P(("dp", "pair")),
            P(("dp", "pair"), None),
            P(("dp", "pair"), None),
        ),
        out_specs=(
            P(("dp", "pair"), None),
            P(("dp", "pair"), None),
            P(None, ("dp", "pair")),
            P(("dp", "pair")),
            P(("dp", "pair")),
            P(("dp", "pair"), None),
        ),
        check_vma=False,
    )
```

profile of v0, /device:TPU:1, one launch (start us, length us, event | category | flops | bytes accessed | tf_op | source)
XLA Modules:
  0.0 1933.7 jit_solution(4667449494425731221)
XLA Ops:
  19.3 68.0 %all-gather = f32[256,6,33]{2,1,0:T(8,128)S(1)} all-gather(f32[1,6,33]{2,1,0:T(8,128)S(1)} %maximum_bitcast_fusion), channel_id=1, replica_groups=mesh['dp'=128,'pair'=2] {'dp','pair'}, dimensions={0}, use_global_device_ids=true | all-gather | bytes 203544 | tf_op jit(solution)/shard_map/all_gather | solution.py:35
  107.4 75.7 %all-reduce.5 = (f32[1536]{0:T(1024)S(1)}, f32[]{:T(128)}) all-reduce(f32[1536]{0:T(1024)S(1)} %get-tuple-element.89, f32[]{:T(128)} %convert_reduce_fusion), channel_id=1, replica_groups=mesh['dp'=128,'pair'=2] {'dp','pair'}, use_global_device_ids=true, to_apply=%region_1.2 | all-reduce | flops 1537 | bytes 12296 | tf_op jit(solution)/shard_map/psum | solution.py:50
  184.0 74.2 %psum.37 = f32[1536]{0:T(1024)S(1)} all-reduce(f32[1536]{0:T(1024)S(1)} %fusion.119), channel_id=1, replica_groups=mesh['dp'=128,'pair'=2] {'dp','pair'}, use_global_device_ids=true, to_apply=%region_5.6 | all-reduce | flops 1536 | bytes 12288 | tf_op jit(solution)/shard_map/psum | solution.py:55
  264.0 709.9 %fusion = f32[8,1536]{1,0:T(8,128)S(1)} fusion(f32[1536,1536]{1,0:T(8,128)} %fusion.124), kind=kCustom, calls=%all-reduce-scatter | all-reduce-scatter fusion | flops 3145729 | bytes 9486336
  1005.7 17.9 collective-permute-start.51
  1066.6 13.1 collective-permute-start.34
  1079.7 13.1 collective-permute-start.33
  1092.9 13.1 collective-permute-start.32
  1106.0 13.1 collective-permute-start.31
  1119.2 13.1 collective-permute-start.30
  1132.3 13.1 collective-permute-start.29
  1145.5 13.1 collective-permute-start.28
  1158.6 13.1 collective-permute-start.27
  1171.8 13.1 collective-permute-start.26
  1184.9 13.1 collective-permute-start.25
  1198.1 13.1 collective-permute-start.24
  1316.4 13.3 collective-permute-start.15
  1408.6 13.7 collective-permute-start.8
  1422.4 13.1 collective-permute-start.7
  1435.5 13.1 collective-permute-start.6
  1448.7 13.1 collective-permute-start.5
  1466.0 97.2 %concatenate.45 = f32[518,1536]{1,0:T(8,128)} concatenate(f32[6,1536]{1,0:T(8,128)S(1)} %collective-permute-done.67, f32[8,1536]{1,0:T(8,128)S(1)} %collective-permute-done.66, f32[8,1536]{1,0:T(8,128)S(1)} %collective-permute-done.65, f32[8,1536]{1,0:T(8,128)S(1)} %collective-permute-done.64, f32[8,1536]{1,0:T(8,128)S(1)} %collective-permute-done.63, ...), dimensions={0} | concatenate | bytes 6365184
  1580.0 79.5 %all-reduce.4 = (f32[1536]{0:T(1024)S(1)}, f32[1536]{0:T(1024)S(1)}) all-reduce(f32[1536]{0:T(1024)S(1)} %get-tuple-element.50, f32[1536]{0:T(1024)S(1)} %get-tuple-element.49), channel_id=1, replica_groups=mesh['dp'=128,'pair'=2] {'dp','pair'}, use_global_device_ids=true, to_apply=%region_9.10 | all-reduce | flops 3072 | bytes 24576 | tf_op jit(solution)/shard_map/psum | solution.py:68
  1688.0 237.1 %all-reduce.8.cloned.1.call-done = f32[31,1536]{1,0:T(8,128)} async-done(((f32[31,1536]{1,0:T(8,128)}), f32[31,1536]{1,0:T(8,128)}) %all-reduce.8.cloned.1.call-update) | async-done | bytes 190480
  (370 shorter events, 346.3 us)
Async XLA Ops:
  7.2 1557.6 %all-gather.4.cloned.1.call-start = ((), (), s32[]{:S(2)}) async-start(), calls=%async_computation | async-start | bytes 6316032 | tf_op jit(solution)/shard_map/all_gather | solution.py:62
  7.9 1917.2 %all-reduce.8.cloned.1.call-start = ((), (), s32[]{:S(2)}) async-start(), calls=%async_computation.1 | async-start | bytes 393216
  9.7 92.7 %collective-permute-start = (bf16[15,1536]{1,0:T(8,128)(2,1)S(1)}, bf16[15,1536]{1,0:T(8,128)(2,1)S(1)}, u32[]{:S(2)}, u32[]{:S(2)}) collective-permute-start(bf16[15,1536]{1,0:T(8,128)(2,1)S(1)} %get-tuple-element.93), channel_id=1, source_target_pairs={{0,1},{1,2},{2,3},{3,4},{4,5},{5,6},{6,7},{7,8},{8,9},{9,10},{10,1... | collective-permute-start | bytes 138248 | tf_op jit(solution)/shard_map/ppermute | solution.py:17
  14.3 88.1 %collective-permute-start.1 = (bf16[15,1536]{1,0:T(8,128)(2,1)S(1)}, bf16[15,1536]{1,0:T(8,128)(2,1)S(1)}, u32[]{:S(2)}, u32[]{:S(2)}) collective-permute-start(bf16[15,1536]{1,0:T(8,128)(2,1)S(1)} %get-tuple-element.94), channel_id=1, source_target_pairs={{1,0},{2,1},{3,2},{4,3},{5,4},{6,5},{7,6},{8,7},{9,8},{10,9},{11,1... | collective-permute-start | bytes 138248 | tf_op jit(solution)/shard_map/ppermute | solution.py:19
  1066.6 65.7 %collective-permute-start.34 = (f32[8,1536]{1,0:T(8,128)S(1)}, f32[8,1536]{1,0:T(8,128)S(1)}, u32[]{:S(2)}, u32[]{:S(2)}) collective-permute-start(f32[8,1536]{1,0:T(8,128)S(1)} %fusion), channel_id=1, source_target_pairs={{0,31},{1,32},{2,33},{3,34},{4,35},{5,36},{6,37},{7,38},{8,39},{9,... | collective-permute-start | bytes 147464
  1079.7 65.7 %collective-permute-start.33 = (f32[8,1536]{1,0:T(8,128)S(1)}, f32[8,1536]{1,0:T(8,128)S(1)}, u32[]{:S(2)}, u32[]{:S(2)}) collective-permute-start(f32[8,1536]{1,0:T(8,128)S(1)} %fusion), channel_id=1, source_target_pairs={{0,30},{1,31},{2,32},{3,33},{4,34},{5,35},{6,36},{7,37},{8,38},{9,... | collective-permute-start | bytes 147464
  1092.9 65.7 %collective-permute-start.32 = (f32[8,1536]{1,0:T(8,128)S(1)}, f32[8,1536]{1,0:T(8,128)S(1)}, u32[]{:S(2)}, u32[]{:S(2)}) collective-permute-start(f32[8,1536]{1,0:T(8,128)S(1)} %fusion), channel_id=1, source_target_pairs={{0,29},{1,30},{2,31},{3,32},{4,33},{5,34},{6,35},{7,36},{8,37},{9,... | collective-permute-start | bytes 147464
  1106.0 65.7 %collective-permute-start.31 = (f32[8,1536]{1,0:T(8,128)S(1)}, f32[8,1536]{1,0:T(8,128)S(1)}, u32[]{:S(2)}, u32[]{:S(2)}) collective-permute-start(f32[8,1536]{1,0:T(8,128)S(1)} %fusion), channel_id=1, source_target_pairs={{0,28},{1,29},{2,30},{3,31},{4,32},{5,33},{6,34},{7,35},{8,36},{9,... | collective-permute-start | bytes 147464
  1119.2 65.7 %collective-permute-start.30 = (f32[8,1536]{1,0:T(8,128)S(1)}, f32[8,1536]{1,0:T(8,128)S(1)}, u32[]{:S(2)}, u32[]{:S(2)}) collective-permute-start(f32[8,1536]{1,0:T(8,128)S(1)} %fusion), channel_id=1, source_target_pairs={{0,27},{1,28},{2,29},{3,30},{4,31},{5,32},{6,33},{7,34},{8,35},{9,... | collective-permute-start | bytes 147464
  1132.3 65.7 %collective-permute-start.29 = (f32[8,1536]{1,0:T(8,128)S(1)}, f32[8,1536]{1,0:T(8,128)S(1)}, u32[]{:S(2)}, u32[]{:S(2)}) collective-permute-start(f32[8,1536]{1,0:T(8,128)S(1)} %fusion), channel_id=1, source_target_pairs={{0,26},{1,27},{2,28},{3,29},{4,30},{5,31},{6,32},{7,33},{8,34},{9,... | collective-permute-start | bytes 147464
  1145.5 65.7 %collective-permute-start.28 = (f32[8,1536]{1,0:T(8,128)S(1)}, f32[8,1536]{1,0:T(8,128)S(1)}, u32[]{:S(2)}, u32[]{:S(2)}) collective-permute-start(f32[8,1536]{1,0:T(8,128)S(1)} %fusion), channel_id=1, source_target_pairs={{0,25},{1,26},{2,27},{3,28},{4,29},{5,30},{6,31},{7,32},{8,33},{9,... | collective-permute-start | bytes 147464
  1158.6 65.7 %collective-permute-start.27 = (f32[8,1536]{1,0:T(8,128)S(1)}, f32[8,1536]{1,0:T(8,128)S(1)}, u32[]{:S(2)}, u32[]{:S(2)}) collective-permute-start(f32[8,1536]{1,0:T(8,128)S(1)} %fusion), channel_id=1, source_target_pairs={{0,24},{1,25},{2,26},{3,27},{4,28},{5,29},{6,30},{7,31},{8,32},{9,... | collective-permute-start | bytes 147464
  1171.8 65.7 %collective-permute-start.26 = (f32[8,1536]{1,0:T(8,128)S(1)}, f32[8,1536]{1,0:T(8,128)S(1)}, u32[]{:S(2)}, u32[]{:S(2)}) collective-permute-start(f32[8,1536]{1,0:T(8,128)S(1)} %fusion), channel_id=1, source_target_pairs={{0,23},{1,24},{2,25},{3,26},{4,27},{5,28},{6,29},{7,30},{8,31},{9,... | collective-permute-start | bytes 147464
  1184.9 65.7 %collective-permute-start.25 = (f32[8,1536]{1,0:T(8,128)S(1)}, f32[8,1536]{1,0:T(8,128)S(1)}, u32[]{:S(2)}, u32[]{:S(2)}) collective-permute-start(f32[8,1536]{1,0:T(8,128)S(1)} %fusion), channel_id=1, source_target_pairs={{0,22},{1,23},{2,24},{3,25},{4,26},{5,27},{6,28},{7,29},{8,30},{9,... | collective-permute-start | bytes 147464
  1198.1 65.7 %collective-permute-start.24 = (f32[8,1536]{1,0:T(8,128)S(1)}, f32[8,1536]{1,0:T(8,128)S(1)}, u32[]{:S(2)}, u32[]{:S(2)}) collective-permute-start(f32[8,1536]{1,0:T(8,128)S(1)} %fusion), channel_id=1, source_target_pairs={{0,21},{1,22},{2,23},{3,24},{4,25},{5,26},{6,27},{7,28},{8,29},{9,... | collective-permute-start | bytes 147464
  1263.8 65.9 %collective-permute-start.19 = (f32[8,1536]{1,0:T(8,128)S(1)}, f32[8,1536]{1,0:T(8,128)S(1)}, u32[]{:S(2)}, u32[]{:S(2)}) collective-permute-start(f32[8,1536]{1,0:T(8,128)S(1)} %fusion), channel_id=1, source_target_pairs={{0,16},{1,17},{2,18},{3,19},{4,20},{5,21},{6,22},{7,23},{8,24},{9,... | collective-permute-start | bytes 147464
  1277.0 65.9 %collective-permute-start.18 = (f32[8,1536]{1,0:T(8,128)S(1)}, f32[8,1536]{1,0:T(8,128)S(1)}, u32[]{:S(2)}, u32[]{:S(2)}) collective-permute-start(f32[8,1536]{1,0:T(8,128)S(1)} %fusion), channel_id=1, source_target_pairs={{0,15},{1,16},{2,17},{3,18},{4,19},{5,20},{6,21},{7,22},{8,23},{9,... | collective-permute-start | bytes 147464
  1290.1 65.9 %collective-permute-start.17 = (f32[8,1536]{1,0:T(8,128)S(1)}, f32[8,1536]{1,0:T(8,128)S(1)}, u32[]{:S(2)}, u32[]{:S(2)}) collective-permute-start(f32[8,1536]{1,0:T(8,128)S(1)} %fusion), channel_id=1, source_target_pairs={{0,14},{1,15},{2,16},{3,17},{4,18},{5,19},{6,20},{7,21},{8,22},{9,... | collective-permute-start | bytes 147464
  1303.3 65.9 %collective-permute-start.16 = (f32[8,1536]{1,0:T(8,128)S(1)}, f32[8,1536]{1,0:T(8,128)S(1)}, u32[]{:S(2)}, u32[]{:S(2)}) collective-permute-start(f32[8,1536]{1,0:T(8,128)S(1)} %fusion), channel_id=1, source_target_pairs={{0,13},{1,14},{2,15},{3,16},{4,17},{5,18},{6,19},{7,20},{8,21},{9,... | collective-permute-start | bytes 147464
  1316.4 65.9 %collective-permute-start.15 = (f32[8,1536]{1,0:T(8,128)S(1)}, f32[8,1536]{1,0:T(8,128)S(1)}, u32[]{:S(2)}, u32[]{:S(2)}) collective-permute-start(f32[8,1536]{1,0:T(8,128)S(1)} %fusion), channel_id=1, source_target_pairs={{0,12},{1,13},{2,14},{3,15},{4,16},{5,17},{6,18},{7,19},{8,20},{9,... | collective-permute-start | bytes 147464
  1356.0 66.3 %collective-permute-start.12 = (f32[8,1536]{1,0:T(8,128)S(1)}, f32[8,1536]{1,0:T(8,128)S(1)}, u32[]{:S(2)}, u32[]{:S(2)}) collective-permute-start(f32[8,1536]{1,0:T(8,128)S(1)} %fusion), channel_id=1, source_target_pairs={{0,9},{1,10},{2,11},{3,12},{4,13},{5,14},{6,15},{7,16},{8,17},{9,1... | collective-permute-start | bytes 147464
  1369.2 66.3 %collective-permute-start.11 = (f32[8,1536]{1,0:T(8,128)S(1)}, f32[8,1536]{1,0:T(8,128)S(1)}, u32[]{:S(2)}, u32[]{:S(2)}) collective-permute-start(f32[8,1536]{1,0:T(8,128)S(1)} %fusion), channel_id=1, source_target_pairs={{0,8},{1,9},{2,10},{3,11},{4,12},{5,13},{6,14},{7,15},{8,16},{9,17... | collective-permute-start | bytes 147464
  1382.3 66.3 %collective-permute-start.10 = (f32[8,1536]{1,0:T(8,128)S(1)}, f32[8,1536]{1,0:T(8,128)S(1)}, u32[]{:S(2)}, u32[]{:S(2)}) collective-permute-start(f32[8,1536]{1,0:T(8,128)S(1)} %fusion), channel_id=1, source_target_pairs={{0,7},{1,8},{2,9},{3,10},{4,11},{5,12},{6,13},{7,14},{8,15},{9,16}... | collective-permute-start | bytes 147464
  1395.5 66.3 %collective-permute-start.9 = (f32[8,1536]{1,0:T(8,128)S(1)}, f32[8,1536]{1,0:T(8,128)S(1)}, u32[]{:S(2)}, u32[]{:S(2)}) collective-permute-start(f32[8,1536]{1,0:T(8,128)S(1)} %fusion), channel_id=1, source_target_pairs={{0,6},{1,7},{2,8},{3,9},{4,10},{5,11},{6,12},{7,13},{8,14},{9,15},... | collective-permute-start | bytes 147464
  (134 other events, 11989.2 us)
Sparse Core Ops, SparseCore 0:
  11.9 120.5 all-gather.3
  1678.2 246.9 all-reduce.7
where the time goes:
time: 1950 us; the launch traced here: 1930 us
  blocking collectives  1010 us (52%)
  starting transfers between devices  502 us (26%)
  waiting for transfers between devices  239 us (12%)
  local copies, waits for them, and re-layouts  129 us (7%)
  other arithmetic  27.6 us (1%)
    unnamed x1, blocking collectives  710 us
    unnamed x65, starting transfers between devices  489 us
    unnamed x67, waiting for transfers between devices  239 us
    unnamed x183, local copies, waits for them, and re-layouts  109 us
    psum x1, blocking collectives, local(): lax.psum((jnp.sum(grad_pre * normed, axis=0), jnp.sum(grad_pre, axis=0)),...  79.5 us
    psum x1, blocking collectives, local(): lax.psum((jnp.sum(weight_col * conv, axis=0), jnp.sum(weight_col)), ('dp'...  75.7 us
    psum x1, blocking collectives, local(): lax.psum(jnp.sum(weight_col * centred * centred, axis=0), ('dp', 'pair'))  74.2 us
    all_gather x1, blocking collectives, local(): params_full = lax.all_gather(stacked, ('dp', 'pair'), axis=1, tiled=True)  68 us
  transfers between devices with their start and end apart: 70, of which 3 were waited for; matrix products, arithmetic and copies ran while one was open for 44% of the time, Pallas kernels for 0%

commit v1 on v0

--- a/solution.py
+++ b/solution.py
@@ -32,7 +32,10 @@
     device_pos = lax.axis_index(("dp", "pair"))
     weight_col = frame_mask.astype(jnp.float32)[:, None]
     stacked = jnp.concatenate([dw_kernel, norm_scale[None, :], norm_shift[None, :]], axis=0)
-    params_full = lax.all_gather(stacked, ("dp", "pair"), axis=1, tiled=True)
+    size = lax.axis_size(("dp", "pair"))
+    tiles = jnp.stack([stacked for _ in range(size)])
+    tiles = lax.all_to_all(tiles, ("dp", "pair"), split_axis=0, concat_axis=0)
+    params_full = jnp.concatenate(tiles, axis=1)
     kernel_full = params_full[:KERNEL]
     scale_full = params_full[KERNEL]
     shift_full = params_full[KERNEL + 1]

time: 1950 us -> 1920 us (0.985)
  blocking collectives: 1010 us -> 937 us
  local copies, waits for them, and re-layouts: 129 us -> 162 us
    all_gather x1 -> x0, blocking collectives: 68 us -> none  [local(): params_full = lax.all_gather(stacked, ('dp', 'pair'), axis=1, tiled=True)]
    mul x0 -> x32, local copies, waits for them, and re-layouts: none -> 21.7 us  [the longest x31 20.7 us: local(): kernel_full[offset] * padded_in[offset:offset + local_rows]]
    unnamed x183 -> x199, local copies, waits for them, and re-layouts: 109 us -> 111 us
  transfers between devices with their start and end apart: 70 -> 71, of which waited for: 3 -> 4; matrix products, arithmetic and copies ran while one was open for 44% -> 47% of each run, Pallas kernels for 0% -> 0%
where the time goes in v1:
time: 1920 us; the launch traced here: 1910 us
  blocking collectives  937 us (49%)
  starting transfers between devices  505 us (26%)
  waiting for transfers between devices  247 us (13%)
  local copies, waits for them, and re-layouts  162 us (8%)
  other arithmetic  34.3 us (2%)
    unnamed x1, blocking collectives  709 us
    unnamed x65, starting transfers between devices  478 us
    unnamed x67, waiting for transfers between devices  239 us
    unnamed x199, local copies, waits for them, and re-layouts  111 us
    psum x1, blocking collectives, local(): lax.psum((jnp.sum(grad_pre * normed, axis=0), jnp.sum(grad_pre, axis=0)),...  79.5 us
    psum x1, blocking collectives, local(): lax.psum(jnp.sum(weight_col * centred * centred, axis=0), ('dp', 'pair'))  74 us
    psum x1, blocking collectives, local(): lax.psum((jnp.sum(weight_col * conv, axis=0), jnp.sum(weight_col)), ('dp'...  73.7 us
  transfers between devices with their start and end apart: 71, of which 4 were waited for; matrix products, arithmetic and copies ran while one was open for 47% of the time, Pallas kernels for 0%

profile of v1, /device:TPU:1, one launch (start us, length us, event | category | flops | bytes accessed | tf_op | source)
XLA Modules:
  0.0 1914.8 jit_solution(2064241873499779715)
XLA Ops:
  19.9 15.0 all-to-all-start
  70.6 14.1 slice_reduce_fusion.32
  103.1 73.7 %all-reduce.5 = (f32[1536]{0:T(1024)S(1)}, f32[]{:T(128)}) all-reduce(f32[1536]{0:T(1024)S(1)} %get-tuple-element.89, f32[]{:T(128)} %convert_reduce_fusion), channel_id=1, replica_groups=mesh['dp'=128,'pair'=2] {'dp','pair'}, use_global_device_ids=true, to_apply=%region_1.2 | all-reduce | flops 1537 | bytes 12296 | tf_op jit(solution)/shard_map/psum | solution.py:53
  177.6 74.0 %psum.37 = f32[1536]{0:T(1024)S(1)} all-reduce(f32[1536]{0:T(1024)S(1)} %fusion.119), channel_id=1, replica_groups=mesh['dp'=128,'pair'=2] {'dp','pair'}, use_global_device_ids=true, to_apply=%region_5.6 | all-reduce | flops 1536 | bytes 12288 | tf_op jit(solution)/shard_map/psum | solution.py:58
  257.4 709.4 %fusion = f32[8,1536]{1,0:T(8,128)S(1)} fusion(f32[1536,1536]{1,0:T(8,128)} %fusion.124), kind=kCustom, calls=%all-reduce-scatter | all-reduce-scatter fusion | flops 3145729 | bytes 9486336
  998.6 17.9 collective-permute-start.51
  1060.8 13.1 collective-permute-start.33
  1074.0 13.1 collective-permute-start.32
  1087.1 13.1 collective-permute-start.31
  1100.3 13.1 collective-permute-start.30
  1113.4 13.1 collective-permute-start.29
  1126.6 13.1 collective-permute-start.28
  1139.7 13.1 collective-permute-start.27
  1152.9 13.1 collective-permute-start.26
  1166.0 13.1 collective-permute-start.25
  1179.2 13.1 collective-permute-start.24
  1192.3 13.1 collective-permute-start.23
  1389.6 13.7 collective-permute-start.8
  1403.3 13.2 collective-permute-start.7
  1416.5 13.1 collective-permute-start.6
  1429.6 13.1 collective-permute-start.5
  1446.9 97.2 %concatenate.45 = f32[518,1536]{1,0:T(8,128)} concatenate(f32[6,1536]{1,0:T(8,128)S(1)} %collective-permute-done.67, f32[8,1536]{1,0:T(8,128)S(1)} %collective-permute-done.66, f32[8,1536]{1,0:T(8,128)S(1)} %collective-permute-done.65, f32[8,1536]{1,0:T(8,128)S(1)} %collective-permute-done.64, f32[8,1536]{1,0:T(8,128)S(1)} %collective-permute-done.63, ...), dimensions={0} | concatenate | bytes 6365184
  1560.9 79.5 %all-reduce.4 = (f32[1536]{0:T(1024)S(1)}, f32[1536]{0:T(1024)S(1)}) all-reduce(f32[1536]{0:T(1024)S(1)} %get-tuple-element.83, f32[1536]{0:T(1024)S(1)} %get-tuple-element.82), channel_id=1, replica_groups=mesh['dp'=128,'pair'=2] {'dp','pair'}, use_global_device_ids=true, to_apply=%region_9.10 | all-reduce | flops 3072 | bytes 24576 | tf_op jit(solution)/shard_map/psum | solution.py:71
  1669.4 236.7 %all-reduce.8.cloned.1.call-done = f32[31,1536]{1,0:T(8,128)} async-done(((f32[31,1536]{1,0:T(8,128)}), f32[31,1536]{1,0:T(8,128)}) %all-reduce.8.cloned.1.call-update) | async-done | bytes 190480
  (423 shorter events, 382.3 us)
Async XLA Ops:
  7.2 1538.4 %all-gather.3.cloned.1.call-start = ((), (), s32[]{:S(2)}) async-start(), calls=%async_computation.1 | async-start | bytes 6316032 | tf_op jit(solution)/shard_map/all_gather | solution.py:65
  35.0 1871.2 %all-reduce.8.cloned.1.call-start = ((), (), s32[]{:S(2)}) async-start(), calls=%async_computation.2 | async-start | bytes 393216
  1060.8 65.7 %collective-permute-start.33 = (f32[8,1536]{1,0:T(8,128)S(1)}, f32[8,1536]{1,0:T(8,128)S(1)}, u32[]{:S(2)}, u32[]{:S(2)}) collective-permute-start(f32[8,1536]{1,0:T(8,128)S(1)} %fusion), channel_id=1, source_target_pairs={{0,30},{1,31},{2,32},{3,33},{4,34},{5,35},{6,36},{7,37},{8,38},{9,... | collective-permute-start | bytes 147464
  1074.0 65.7 %collective-permute-start.32 = (f32[8,1536]{1,0:T(8,128)S(1)}, f32[8,1536]{1,0:T(8,128)S(1)}, u32[]{:S(2)}, u32[]{:S(2)}) collective-permute-start(f32[8,1536]{1,0:T(8,128)S(1)} %fusion), channel_id=1, source_target_pairs={{0,29},{1,30},{2,31},{3,32},{4,33},{5,34},{6,35},{7,36},{8,37},{9,... | collective-permute-start | bytes 147464
  1087.1 65.7 %collective-permute-start.31 = (f32[8,1536]{1,0:T(8,128)S(1)}, f32[8,1536]{1,0:T(8,128)S(1)}, u32[]{:S(2)}, u32[]{:S(2)}) collective-permute-start(f32[8,1536]{1,0:T(8,128)S(1)} %fusion), channel_id=1, source_target_pairs={{0,28},{1,29},{2,30},{3,31},{4,32},{5,33},{6,34},{7,35},{8,36},{9,... | collective-permute-start | bytes 147464
  1100.3 65.7 %collective-permute-start.30 = (f32[8,1536]{1,0:T(8,128)S(1)}, f32[8,1536]{1,0:T(8,128)S(1)}, u32[]{:S(2)}, u32[]{:S(2)}) collective-permute-start(f32[8,1536]{1,0:T(8,128)S(1)} %fusion), channel_id=1, source_target_pairs={{0,27},{1,28},{2,29},{3,30},{4,31},{5,32},{6,33},{7,34},{8,35},{9,... | collective-permute-start | bytes 147464
  1113.4 65.7 %collective-permute-start.29 = (f32[8,1536]{1,0:T(8,128)S(1)}, f32[8,1536]{1,0:T(8,128)S(1)}, u32[]{:S(2)}, u32[]{:S(2)}) collective-permute-start(f32[8,1536]{1,0:T(8,128)S(1)} %fusion), channel_id=1, source_target_pairs={{0,26},{1,27},{2,28},{3,29},{4,30},{5,31},{6,32},{7,33},{8,34},{9,... | collective-permute-start | bytes 147464
  1126.6 65.7 %collective-permute-start.28 = (f32[8,1536]{1,0:T(8,128)S(1)}, f32[8,1536]{1,0:T(8,128)S(1)}, u32[]{:S(2)}, u32[]{:S(2)}) collective-permute-start(f32[8,1536]{1,0:T(8,128)S(1)} %fusion), channel_id=1, source_target_pairs={{0,25},{1,26},{2,27},{3,28},{4,29},{5,30},{6,31},{7,32},{8,33},{9,... | collective-permute-start | bytes 147464
  1139.7 65.7 %collective-permute-start.27 = (f32[8,1536]{1,0:T(8,128)S(1)}, f32[8,1536]{1,0:T(8,128)S(1)}, u32[]{:S(2)}, u32[]{:S(2)}) collective-permute-start(f32[8,1536]{1,0:T(8,128)S(1)} %fusion), channel_id=1, source_target_pairs={{0,24},{1,25},{2,26},{3,27},{4,28},{5,29},{6,30},{7,31},{8,32},{9,... | collective-permute-start | bytes 147464
  1152.9 65.7 %collective-permute-start.26 = (f32[8,1536]{1,0:T(8,128)S(1)}, f32[8,1536]{1,0:T(8,128)S(1)}, u32[]{:S(2)}, u32[]{:S(2)}) collective-permute-start(f32[8,1536]{1,0:T(8,128)S(1)} %fusion), channel_id=1, source_target_pairs={{0,23},{1,24},{2,25},{3,26},{4,27},{5,28},{6,29},{7,30},{8,31},{9,... | collective-permute-start | bytes 147464
  1166.0 65.7 %collective-permute-start.25 = (f32[8,1536]{1,0:T(8,128)S(1)}, f32[8,1536]{1,0:T(8,128)S(1)}, u32[]{:S(2)}, u32[]{:S(2)}) collective-permute-start(f32[8,1536]{1,0:T(8,128)S(1)} %fusion), channel_id=1, source_target_pairs={{0,22},{1,23},{2,24},{3,25},{4,26},{5,27},{6,28},{7,29},{8,30},{9,... | collective-permute-start | bytes 147464
  1179.2 65.7 %collective-permute-start.24 = (f32[8,1536]{1,0:T(8,128)S(1)}, f32[8,1536]{1,0:T(8,128)S(1)}, u32[]{:S(2)}, u32[]{:S(2)}) collective-permute-start(f32[8,1536]{1,0:T(8,128)S(1)} %fusion), channel_id=1, source_target_pairs={{0,21},{1,22},{2,23},{3,24},{4,25},{5,26},{6,27},{7,28},{8,29},{9,... | collective-permute-start | bytes 147464
  1192.3 65.7 %collective-permute-start.23 = (f32[8,1536]{1,0:T(8,128)S(1)}, f32[8,1536]{1,0:T(8,128)S(1)}, u32[]{:S(2)}, u32[]{:S(2)}) collective-permute-start(f32[8,1536]{1,0:T(8,128)S(1)} %fusion), channel_id=1, source_target_pairs={{0,20},{1,21},{2,22},{3,23},{4,24},{5,25},{6,26},{7,27},{8,28},{9,... | collective-permute-start | bytes 147464
  1205.5 65.7 %collective-permute-start.22 = (f32[8,1536]{1,0:T(8,128)S(1)}, f32[8,1536]{1,0:T(8,128)S(1)}, u32[]{:S(2)}, u32[]{:S(2)}) collective-permute-start(f32[8,1536]{1,0:T(8,128)S(1)} %fusion), channel_id=1, source_target_pairs={{0,19},{1,20},{2,21},{3,22},{4,23},{5,24},{6,25},{7,26},{8,27},{9,... | collective-permute-start | bytes 147464
  1218.6 65.7 %collective-permute-start.21 = (f32[8,1536]{1,0:T(8,128)S(1)}, f32[8,1536]{1,0:T(8,128)S(1)}, u32[]{:S(2)}, u32[]{:S(2)}) collective-permute-start(f32[8,1536]{1,0:T(8,128)S(1)} %fusion), channel_id=1, source_target_pairs={{0,18},{1,19},{2,20},{3,21},{4,22},{5,23},{6,24},{7,25},{8,26},{9,... | collective-permute-start | bytes 147464
  1231.8 65.7 %collective-permute-start.20 = (f32[8,1536]{1,0:T(8,128)S(1)}, f32[8,1536]{1,0:T(8,128)S(1)}, u32[]{:S(2)}, u32[]{:S(2)}) collective-permute-start(f32[8,1536]{1,0:T(8,128)S(1)} %fusion), channel_id=1, source_target_pairs={{0,17},{1,18},{2,19},{3,20},{4,21},{5,22},{6,23},{7,24},{8,25},{9,... | collective-permute-start | bytes 147464
  1244.9 65.7 %collective-permute-start.19 = (f32[8,1536]{1,0:T(8,128)S(1)}, f32[8,1536]{1,0:T(8,128)S(1)}, u32[]{:S(2)}, u32[]{:S(2)}) collective-permute-start(f32[8,1536]{1,0:T(8,128)S(1)} %fusion), channel_id=1, source_target_pairs={{0,16},{1,17},{2,18},{3,19},{4,20},{5,21},{6,22},{7,23},{8,24},{9,... | collective-permute-start | bytes 147464
  1258.1 65.7 %collective-permute-start.18 = (f32[8,1536]{1,0:T(8,128)S(1)}, f32[8,1536]{1,0:T(8,128)S(1)}, u32[]{:S(2)}, u32[]{:S(2)}) collective-permute-start(f32[8,1536]{1,0:T(8,128)S(1)} %fusion), channel_id=1, source_target_pairs={{0,15},{1,16},{2,17},{3,18},{4,19},{5,20},{6,21},{7,22},{8,23},{9,... | collective-permute-start | bytes 147464
  1271.2 65.7 %collective-permute-start.17 = (f32[8,1536]{1,0:T(8,128)S(1)}, f32[8,1536]{1,0:T(8,128)S(1)}, u32[]{:S(2)}, u32[]{:S(2)}) collective-permute-start(f32[8,1536]{1,0:T(8,128)S(1)} %fusion), channel_id=1, source_target_pairs={{0,14},{1,15},{2,16},{3,17},{4,18},{5,19},{6,20},{7,21},{8,22},{9,... | collective-permute-start | bytes 147464
  1284.4 65.7 %collective-permute-start.16 = (f32[8,1536]{1,0:T(8,128)S(1)}, f32[8,1536]{1,0:T(8,128)S(1)}, u32[]{:S(2)}, u32[]{:S(2)}) collective-permute-start(f32[8,1536]{1,0:T(8,128)S(1)} %fusion), channel_id=1, source_target_pairs={{0,13},{1,14},{2,15},{3,16},{4,17},{5,18},{6,19},{7,20},{8,21},{9,... | collective-permute-start | bytes 147464
  1337.0 66.3 %collective-permute-start.12 = (f32[8,1536]{1,0:T(8,128)S(1)}, f32[8,1536]{1,0:T(8,128)S(1)}, u32[]{:S(2)}, u32[]{:S(2)}) collective-permute-start(f32[8,1536]{1,0:T(8,128)S(1)} %fusion), channel_id=1, source_target_pairs={{0,9},{1,10},{2,11},{3,12},{4,13},{5,14},{6,15},{7,16},{8,17},{9,1... | collective-permute-start | bytes 147464
  1350.1 66.3 %collective-permute-start.11 = (f32[8,1536]{1,0:T(8,128)S(1)}, f32[8,1536]{1,0:T(8,128)S(1)}, u32[]{:S(2)}, u32[]{:S(2)}) collective-permute-start(f32[8,1536]{1,0:T(8,128)S(1)} %fusion), channel_id=1, source_target_pairs={{0,8},{1,9},{2,10},{3,11},{4,12},{5,13},{6,14},{7,15},{8,16},{9,17... | collective-permute-start | bytes 147464
  1363.3 66.3 %collective-permute-start.10 = (f32[8,1536]{1,0:T(8,128)S(1)}, f32[8,1536]{1,0:T(8,128)S(1)}, u32[]{:S(2)}, u32[]{:S(2)}) collective-permute-start(f32[8,1536]{1,0:T(8,128)S(1)} %fusion), channel_id=1, source_target_pairs={{0,7},{1,8},{2,9},{3,10},{4,11},{5,12},{6,13},{7,14},{8,15},{9,16}... | collective-permute-start | bytes 147464
  1376.4 66.3 %collective-permute-start.9 = (f32[8,1536]{1,0:T(8,128)S(1)}, f32[8,1536]{1,0:T(8,128)S(1)}, u32[]{:S(2)}, u32[]{:S(2)}) collective-permute-start(f32[8,1536]{1,0:T(8,128)S(1)} %fusion), channel_id=1, source_target_pairs={{0,6},{1,7},{2,8},{3,9},{4,10},{5,11},{6,12},{7,13},{8,14},{9,15},... | collective-permute-start | bytes 147464
  (142 other events, 11090.1 us)
Sparse Core Ops, SparseCore 0:
  11.9 121.0 all-gather.2
  1659.1 246.9 all-reduce.7
